TPU v7x, 32 devices: a whole 2x2x4 slice. The times are simulated.
32 devices in a mesh: groups: 2 (over y), wide: 8 (over z, x), tp: 2 (over core).
Axes of the slice: x: 2, y: 2, z: 4, core: 2. Of those that a mesh axis runs over, the one named last changes fastest.
Arguments:
- pre_codes: bfloat16 [64, 4, 4, 2, 512], P(('groups', 'wide'), None, 'tp'), parts along dimension 0, may hold values from -6 to 6
- pre_scales: bfloat16 [64, 4, 4, 2, 4], P(('groups', 'wide'), None, 'tp'), parts along dimension 0, may hold values from 0.099609375 to 1
- req_dest: int32 [64], P(('groups', 'wide')), parts along dimension 0, may hold values from 0 to 7, as said below
- req_blocks: int32 [64], P(('groups', 'wide')), parts along dimension 0, may hold values from 1 to 4, as said below
- res_codes: bfloat16 [128, 64, 2, 512], P(('groups', 'wide'), None, None, 'tp'), parts along dimension 0, may hold values from -6 to 6
- res_scales: bfloat16 [128, 64, 2, 4], P(('groups', 'wide'), None, None, 'tp'), parts along dimension 0, may hold values from 0.099609375 to 1
- res_len: int32 [128], P(('groups', 'wide')), parts along dimension 0, may hold values from 1 to 64, as said below
- res_query: bfloat16 [128, 2, 8192], P(('groups', 'wide'), None, 'tp'), parts along dimension 0, may hold values from -128 to 128
- res_new: bfloat16 [128, 2, 2, 512], P(('groups', 'wide'), None, None, 'tp'), parts along dimension 0, may hold values from -6 to 6
- arr_query: bfloat16 [96, 2, 8192], P(('groups', 'wide'), None, 'tp'), parts along dimension 0, may hold values from -128 to 128
- arr_new: bfloat16 [96, 2, 2, 512], P(('groups', 'wide'), None, None, 'tp'), parts along dimension 0, may hold values from -6 to 6
Outputs:
- res_out: bfloat16 [128, 2, 8192], P(('groups', 'wide'), None, 'tp'), parts along dimension 0
- arr_out: bfloat16 [96, 2, 8192], P(('groups', 'wide'), None, 'tp'), parts along dimension 0
There are 2 independent parts, one for each index of `groups`. A program takes and returns all parts, laid end to end along the dimension named above; each array names one. Nothing has to cross between parts.
Inputs may be any that keep to these rules, and one draw needn't show every extreme that they name: `req_dest`: each prefill instance sends at most one request to one decode instance; each decode instance receives at least 2 and at most 6 requests, and some decode instance receives 6 in every draw. For every even r, request r of each prefill instance goes to the instance a fixed distance away along the axis, the same distance for all prefill instances, and request r + 1 to the instance at one of two further such distances. `req_blocks`: some request holds 4 blocks in every draw. `res_len`: some resident request has 64 tokens in every draw.
All inputs are finite; a program needn't handle non-finite values.
Results may differ from a plain program's by a relative error of at most 0.0032.
Values may be sent and summed in bfloat16 or wider, within the bound.
No kernel may reach another device: no remote copies, remote signals or barrier semaphores. Data moves between devices by JAX's collectives and lax.ppermute only.
A program may use at most 64 MiB of HBM per device.

v0:
```python
import functools
import math

import jax
import jax.numpy as jnp
from jax import lax
from jax.experimental import pallas as pl
from jax.experimental.pallas import tpu as pltpu
from jax.sharding import PartitionSpec as P

KVH = 4
HD = 128
HQ = 64
GROUP = HQ // KVH
STEPS = 2

NEGATIVE = -1e30
EMPTY = 1024.0
SCORE_SCALE = 1.0 / math.sqrt(HD)

BF16 = jnp.bfloat16
F32 = jnp.float32


def iota(shape, axis):
    return lax.broadcasted_iota(jnp.int32, shape, axis)


def over(x, n):
    return jnp.right_shift(x, n.bit_length() - 1) if n & (n - 1) == 0 else x // n


def mod(x, n):
    return jnp.bitwise_and(x, n - 1) if n & (n - 1) == 0 else x % n


def dot_nt(a, b):
    return lax.dot_general(a, b, (((1,), (1,)), ((), ())), preferred_element_type=F32)


def dot_nn(a, b):
    return lax.dot_general(a, b, (((1,), (0,)), ((), ())), preferred_element_type=F32)


def top_of(*parts):
    return functools.reduce(jnp.maximum, [jnp.max(p, axis=1, keepdims=True) for p in parts])


def sum_of(*parts):
    return functools.reduce(jnp.add, [jnp.sum(p, axis=1, keepdims=True) for p in parts])


def to_values(weights):
    tiles = [pltpu.roll(weights[:, c : c + HD], 1, 1) for c in range(0, weights.shape[1], HD)]
    return jnp.concatenate(tiles, axis=1).astype(BF16)


def values_up(rows):
    return pltpu.roll(rows.astype(F32), rows.shape[0] - 1, 0).astype(BF16)


def pack_kernel(
    tp, chips, heads, block_rows, dest_hbm, blocks_hbm, codes_hbm, scales_hbm, send_hbm,
    dest_ref, blocks_ref, codes_ref, scales_ref, empty_ref, values_ref, sems, out_sems,
):
    requests, all_rows = codes_ref.shape[:2]
    pairs = [
        (codes_hbm, codes_ref), (scales_hbm, scales_ref),
        (dest_hbm, dest_ref), (blocks_hbm, blocks_ref), (empty_ref, send_hbm),
    ]
    copies = [pltpu.make_async_copy(a, b, sems.at[i]) for i, (a, b) in enumerate(pairs)]
    for copy in copies[:-1]:
        copy.start()
    empty_ref[...] = jnp.full(empty_ref.shape, EMPTY, BF16)
    copies[-1].start()
    rows = all_rows // heads
    per_core = heads // tp
    row_block = over(iota((rows, HD), 0), block_rows)
    to_row = iota((all_rows, all_rows), 0)
    from_row = iota((all_rows, all_rows), 1)
    source = over(mod(to_row, rows), 2) * (2 * heads) + over(to_row, rows) * 2 + mod(to_row, 2)
    by_head = jnp.where(from_row == source, 1.0, 0.0).astype(BF16)
    for copy in copies:
        copy.wait()

    def hand_out(r):
        there = dest_ref[r]
        if chips is not None:
            there = functools.reduce(
                jnp.add, [jnp.where(there == w, p, 0) for p, w in enumerate(chips)]
            )
        target = send_hbm.at[pl.ds(there * tp, tp)]
        return pltpu.make_async_copy(values_ref.at[r], target, out_sems.at[r])

    def place(r):
        held = row_block < blocks_ref[r]
        codes = dot_nn(by_head, codes_ref[r])
        scales = scales_ref[r].astype(F32)
        for j in range(heads):
            values = codes[j * rows : (j + 1) * rows] * scales[:, j : j + 1]
            values = jnp.where(held, values, EMPTY).astype(BF16)
            values_ref[r, tp - 1 - j // per_core, j % per_core] = values

    if requests <= 8:
        for r in range(requests):
            place(r)
        outs = [hand_out(r) for r in range(requests)]
        for out in outs:
            out.start()
        for out in outs:
            out.wait()
    else:
        pl.loop(0, requests)(place)
        pl.loop(0, requests)(lambda r: hand_out(r).start())
        pl.loop(0, requests)(lambda r: hand_out(r).wait())


def resident_kernel(
    len_hbm, codes_hbm, scales_hbm, query_hbm, new_hbm, out_ref,
    len_ref, codes_ref, scales_ref, query_ref, new_ref, sems,
):
    pairs = [
        (query_hbm, query_ref), (new_hbm, new_ref), (scales_hbm, scales_ref),
        (len_hbm, len_ref), (codes_hbm, codes_ref),
    ]
    copies = [pltpu.make_async_copy(a, b, sems.at[i]) for i, (a, b) in enumerate(pairs)]
    for copy in copies:
        copy.start()
    slots, rows = codes_ref.shape[:2]
    heads = scales_ref.shape[2]
    tokens = rows // (2 * heads)
    queries = query_ref.shape[1]
    new_rows = new_ref.shape[0]

    row = iota((rows, HD), 0)
    source = (mod(row, 2) * heads + mod(over(row, 2), heads)) * tokens + over(row, 2 * heads)
    lane = iota((rows, HD), 1)
    spread = jnp.concatenate(
        [jnp.where(source == lane + c, 1.0, 0.0).astype(BF16) for c in range(0, rows, HD)],
        axis=1,
    )
    for copy in copies[:-1]:
        copy.wait()
    flat = jnp.concatenate(
        [scales_ref[:, p, h] for p in range(2) for h in range(heads)], axis=1
    )
    columns = dot_nt(spread, flat).astype(BF16)

    col = iota((queries, rows), 1)
    row_head = over(iota((queries, rows), 0), queries // heads)
    is_key = (mod(col, 2) == 0) & (mod(over(col, 2), heads) == row_head)
    col_token = jnp.where(is_key, over(col, 2 * heads), tokens)

    new_col = iota((queries, new_rows), 1)
    new_row = iota((queries, new_rows), 0)
    new_ok = (
        (mod(new_col, 2) == 0)
        & (mod(over(new_col, 2), heads) == over(new_row, queries // heads))
        & (mod(over(new_col, 2 * heads), STEPS) <= mod(new_row, STEPS))
    )
    new_slot = jnp.where(new_ok, over(new_col, 2 * heads * STEPS), slots)

    every = range(slots)
    new = new_ref[...]
    new_all = dot_nt(query_ref[...].reshape(slots * queries, HD), new)
    copies[-1].wait()
    caches = [codes_ref[s] * columns[:, s : s + 1] for s in every]
    scores = [dot_nt(query_ref[s], caches[s]) for s in every]
    scores = [jnp.where(col_token < len_ref[s], scores[s] * SCORE_SCALE, NEGATIVE) for s in every]
    new_scores = [
        jnp.where(new_slot == s, new_all[s * queries : (s + 1) * queries] * SCORE_SCALE, NEGATIVE)
        for s in every
    ]
    top = [top_of(scores[s], new_scores[s]) for s in every]
    weights = [jnp.exp(scores[s] - top[s]) for s in every]
    new_weights = [jnp.exp(new_scores[s] - top[s]) for s in every]
    total = [sum_of(weights[s], new_weights[s]) for s in every]
    new_mixed = dot_nn(jnp.concatenate(new_weights, axis=0).astype(BF16), values_up(new))
    mixed = [
        dot_nn(to_values(weights[s]), caches[s]) + new_mixed[s * queries : (s + 1) * queries]
        for s in every
    ]
    for s in every:
        out_ref[s] = (mixed[s] * (1.0 / total[s])).astype(BF16)


def slots_by_rows(got_ref, tp, order, block_rows):
    chunk_rows = got_ref.shape[2]
    blocks = chunk_rows // block_rows
    rows = [got_ref[k, 0].astype(F32) for k in range(len(order))]
    here = {
        core // tp: jnp.where(x[:1] < EMPTY, 1.0, 0.0)
        for core, x in zip(order, rows)
        if core % tp == 0
    }
    ranks = {
        w: sum([here[v] for v in here if v < w], jnp.zeros((1, HD), F32)) for w in here
    }
    lane = iota((1, HD), 1)
    block = over(lane, block_rows)
    block = jnp.where(mod(lane, 2) == 0, block, -1)
    per_tile = HD // chunk_rows
    tiles = []
    for start in range(0, len(order), per_tile):
        tile = jnp.full((1, HD), -1.0, F32)
        for i in range(per_tile):
            x, rank = rows[start + i], ranks[order[start + i] // tp]
            for b in range(blocks):
                at = b * block_rows
                value = jnp.where(x[at : at + 1] < EMPTY, rank, -1.0)
                tile = jnp.where(block == i * blocks + b, value, tile)
        tiles.append(tile)
    return jnp.concatenate(tiles, axis=1)


def slots_by_matmul(got_ref, tp):
    chunks, _, chunk_rows = got_ref.shape[:3]
    columns = chunks * chunk_rows
    sender_rows = tp * chunk_rows
    piece = min(columns, 256)
    sums = dot_nt(jnp.ones((16, HD), BF16), got_ref[:, 0].reshape(columns, HD))[:8]
    col = iota((8, columns), 1)
    held = sums < EMPTY
    first = jnp.where(held & (mod(col, sender_rows) == 0), 1.0, 0.0).astype(BF16)
    row = over(iota((piece, piece), 0), sender_rows)
    before = jnp.where(row < over(iota((piece, piece), 1), sender_rows), 1.0, 0.0).astype(BF16)
    base = jnp.zeros((8, 1), F32)
    ranks = []
    for p in range(0, columns, piece):
        part = first[:, p : p + piece]
        ranks.append(dot_nn(part, before) + base)
        base = base + jnp.sum(part.astype(F32), axis=1, keepdims=True)
    rank = jnp.concatenate(ranks, axis=1)
    return jnp.where(held & (mod(col, 2) == 0), rank, -1.0)[:1]


def arrival_kernel(
    tp, groups, order, block_rows, got_ref, query_ref, new_ref, out_ref
):
    step = pl.program_id(0) if groups > 1 else 0
    chunks, heads, chunk_rows = got_ref.shape[:3]
    slots, _, per_head = query_ref.shape[:3]
    rows = slots * per_head
    columns = chunks * chunk_rows
    every = range(heads)

    caches = [got_ref[:, h].reshape(columns, HD) for h in every]
    queries = [query_ref[:, h].reshape(rows, HD) for h in every]
    new = new_ref[...]
    scores = [dot_nt(queries[h], caches[h]) for h in every]
    new_all = dot_nt(jnp.concatenate(queries, axis=0), new)
    if order is None:
        slot_of = slots_by_matmul(got_ref, tp)
    else:
        slot_of = slots_by_rows(got_ref, tp, order, block_rows)
    first_slot = jnp.float32(step * slots)
    mine = [slot_of == first_slot + a for a in range(slots)]

    new_col = iota((rows, new.shape[0]), 1)
    new_row = iota((rows, new.shape[0]), 0)
    new_here = (
        (mod(new_col, 2) == 0)
        & (over(new_col, 2 * heads * STEPS) == over(new_row, per_head))
        & (mod(over(new_col, 2 * heads), STEPS) <= mod(new_row, STEPS))
    )
    new_head = jnp.where(new_here, mod(over(new_col, 2), heads), heads)

    scores = [
        jnp.concatenate(
            [
                jnp.where(mine[a], scores[h][a * per_head : (a + 1) * per_head] * SCORE_SCALE, NEGATIVE)
                for a in range(slots)
            ],
            axis=0,
        )
        for h in every
    ]
    new_scores = [
        jnp.where(new_head == h, new_all[h * rows : (h + 1) * rows] * SCORE_SCALE, NEGATIVE)
        for h in every
    ]
    top = [top_of(scores[h], new_scores[h]) for h in every]
    weights = [jnp.exp(scores[h] - top[h]) for h in every]
    new_weights = [jnp.exp(new_scores[h] - top[h]) for h in every]
    total = [sum_of(weights[h], new_weights[h]) for h in every]
    new_mixed = dot_nn(jnp.concatenate(new_weights, axis=0).astype(BF16), values_up(new))
    for h in every:
        mixed = dot_nn(to_values(weights[h]), caches[h]) + new_mixed[h * rows : (h + 1) * rows]
        out_ref[:, h] = (mixed * (1.0 / total[h])).astype(BF16).reshape(slots, per_head, HD)


def whole(memory_space=pltpu.VMEM):
    return pl.BlockSpec(memory_space=memory_space)


def in_hbm(x):
    return pltpu.with_memory_space_constraint(x, pltpu.HBM)


def limit(mib):
    return pltpu.CompilerParams(vmem_limit_bytes=mib * 2**20)


def pack(pre_codes, pre_scales, req_dest, req_blocks, peers, tp, chips):
    requests, blocks, block_tokens = pre_codes.shape[:3]
    tokens = blocks * block_tokens
    codes = (
        pre_codes.reshape(requests, tokens, 2, KVH, HD)
        .transpose(0, 1, 3, 2, 4)
        .reshape(requests, tokens * KVH * 2, HD)
    )
    scales = pre_scales.reshape(requests, tokens * 2, KVH)
    ins = [req_dest, req_blocks, codes, scales]
    chunk = (KVH // tp, tokens * 2, HD)
    return pl.pallas_call(
        functools.partial(pack_kernel, tp, chips, KVH, 2 * block_tokens),
        out_shape=jax.ShapeDtypeStruct((peers * tp,) + chunk, BF16),
        in_specs=[whole(pltpu.HBM)] * len(ins),
        out_specs=whole(pltpu.HBM),
        scratch_shapes=[
            pltpu.SMEM(req_dest.shape, jnp.int32),
            pltpu.SMEM(req_blocks.shape, jnp.int32),
            pltpu.VMEM(codes.shape, BF16),
            pltpu.VMEM(scales.shape, BF16),
            pltpu.VMEM((peers * tp,) + chunk, BF16),
            pltpu.VMEM((requests, tp) + chunk, BF16),
            pltpu.SemaphoreType.DMA((5,)),
            pltpu.SemaphoreType.DMA((requests,)),
        ],
        compiler_params=limit(24),
        name="pack",
    )(*[in_hbm(x) for x in ins])


def cache_rows(codes):
    slots, tokens, _, width = codes.shape
    heads = width // HD
    return (
        codes.reshape(slots, tokens, 2, heads, HD)
        .transpose(0, 1, 3, 2, 4)
        .reshape(slots, tokens * heads * 2, HD)
    )


def query_rows(query):
    slots, steps, width = query.shape
    return query.reshape(slots, steps, width // HD, HD).transpose(0, 2, 1, 3)


def new_rows_of(new):
    slots, steps, pair, width = new.shape
    heads = width // HD
    return (
        new.reshape(slots, steps, pair, heads, HD)
        .transpose(0, 1, 3, 2, 4)
        .reshape(slots * steps * heads * pair, HD)
    )


def from_rows(out, shape):
    slots, steps, width = shape
    return out.reshape(slots, width // HD, steps, HD).transpose(0, 2, 1, 3).reshape(shape)


def resident(codes, res_scales, res_len, res_query, res_new):
    slots, rows = codes.shape[:2]
    heads = res_scales.shape[-1]
    scales = res_scales.transpose(0, 2, 3, 1)
    query = query_rows(res_query).reshape(slots, heads * GROUP * STEPS, HD)
    ins = [res_len, codes, scales, query, new_rows_of(res_new)]
    work = query.shape[0] * query.shape[1] * rows
    return pl.pallas_call(
        resident_kernel,
        out_shape=jax.ShapeDtypeStruct(query.shape, BF16),
        in_specs=[whole(pltpu.HBM)] * len(ins),
        out_specs=whole(),
        scratch_shapes=[
            pltpu.SMEM(res_len.shape, jnp.int32),
            *[pltpu.VMEM(x.shape, BF16) for x in ins[1:]],
            pltpu.SemaphoreType.DMA((len(ins),)),
        ],
        cost_estimate=pl.CostEstimate(
            flops=4 * work * HD,
            bytes_accessed=2 * (codes.size + 2 * query.size),
            transcendentals=work,
        ),
        compiler_params=limit(16),
        name="resident",
    )(*[in_hbm(x) for x in ins])


def arrivals(got, arr_query, arr_new, tp, order, block_rows):
    slots, steps, width = arr_query.shape
    heads = width // (HD * GROUP)
    query = query_rows(arr_query).reshape(slots, heads, GROUP * steps, HD)
    new = new_rows_of(arr_new)
    size = max(n for n in range(1, 7) if slots % n == 0)
    groups = slots // size
    small = got.size <= 2**18

    def part(ref, rows):
        if groups == 1:
            return whole()
        return pl.BlockSpec((rows,) + ref.shape[1:], lambda i: (i,) + (0,) * (ref.ndim - 1))

    return pl.pallas_call(
        functools.partial(arrival_kernel, tp, groups, order, block_rows),
        out_shape=jax.ShapeDtypeStruct(query.shape, BF16),
        grid=(groups,) if groups > 1 else (),
        in_specs=[whole(), part(query, size), part(new, new.shape[0] // groups)],
        out_specs=part(query, size),
        compiler_params=limit(16 if small else 48),
        name="arrivals",
    )(got, query, new)


def shards(
    pre_codes,
    pre_scales,
    req_dest,
    req_blocks,
    res_codes,
    res_scales,
    res_len,
    res_query,
    res_new,
    arr_query,
    arr_new,
):
    peers = lax.axis_size("wide")
    tp = lax.axis_size("tp")
    chips = [5, 6, 7, 1, 0, 2, 3, 4] if peers == 8 else None
    cores = [w * tp + t for w in chips or range(peers) for t in reversed(range(tp))]
    order = chips and cores
    send = pack(pre_codes, pre_scales, req_dest, req_blocks, peers, tp, chips)
    got = lax.all_to_all(
        send,
        ("wide", "tp"),
        split_axis=0,
        concat_axis=0,
        tiled=True,
        axis_index_groups=[cores],
    )
    res_out = resident(cache_rows(res_codes), res_scales, res_len, res_query, res_new)
    block_rows = 2 * pre_codes.shape[2]
    arr_out = arrivals(got, arr_query, arr_new, tp, order, block_rows)
    return (from_rows(res_out, res_query.shape), from_rows(arr_out, arr_query.shape))


def solution(mesh):
    in_specs = (
        P(("groups", "wide"), None, "tp", None, None),
        P(("groups", "wide"), None, "tp", None, None),
        P(("groups", "wide")),
        P(("groups", "wide")),
        P(("groups", "wide"), None, None, "tp"),
        P(("groups", "wide"), None, None, "tp"),
        P(("groups", "wide")),
        P(("groups", "wide"), None, "tp"),
        P(("groups", "wide"), None, None, "tp"),
        P(("groups", "wide"), None, "tp"),
        P(("groups", "wide"), None, None, "tp"),
    )
    out_specs = (P(("groups", "wide"), None, "tp"), P(("groups", "wide"), None, "tp"))
    return jax.shard_map(shards, mesh=mesh, in_specs=in_specs, out_specs=out_specs, check_vma=False)
```

profile of v0, /device:TPU:1, one launch (start us, length us, event | category | flops | bytes accessed | tf_op | source)
XLA Modules:
  0.0 15.1 jit_solution(17444041270394070641)
XLA Ops:
  0.6 1.7 %pack.1 = bf16[16,2,16,128]{3,2,1,0:T(8,128)(2,1)} custom-call(s32[4]{0:T(128)} %dest_hbm.1, s32[4]{0:T(128)} %blocks_hbm.1, bf16[4,64,128]{2,1,0:T(8,128)(2,1)} %bitcast.48, bf16[4,16,4]{2,1,0:T(8,128)(2,1)} %bitcast.50), custom_call_target="tpu_custom_call" | custom-call | tf_op jit(solution)/shard_map/pack/pallas_call | solution.py:315
  2.4 7.4 %all-to-all-start = ((bf16[16,2,16,128]{3,2,1,0:T(8,128)(2,1)}), bf16[16,2,16,128]{3,2,1,0:T(8,128)(2,1)S(1)}, u32[]{:S(2)}, u32[]{:S(2)}) async-start(bf16[16,2,16,128]{3,2,1,0:T(8,128)(2,1)} %pack.1), calls=%async_computation | async-start | bytes 262144 | tf_op jit(solution)/shard_map/all_to_all | solution.py:436
  9.8 0.0 copy-start
  9.8 0.0 copy-start.1
  9.8 2.8 %resident.1 = bf16[8,64,128]{2,1,0:T(8,128)(2,1)} custom-call(s32[8]{0:T(128)} %len_hbm.1, bf16[8,256,128]{2,1,0:T(8,128)(2,1)} %bitcast.44, bf16[8,2,2,64]{3,2,1,0:T(2,128)(2,1)} %bitcast.51, bf16[8,64,128]{2,1,0:T(8,128)(2,1)} %bitcast.45, bf16[64,128]{1,0:T(8,128)(2,1)} %bitcast.49), custom_call_target="tpu_custom_call" | custom-call | flops 67108864 | bytes 786432 | tf_op jit(solution)/shard_map/resident/pallas_call | solution.py:372
  12.6 1.2 %all-to-all-done.got_ref = bf16[16,2,16,128]{3,2,1,0:T(8,128)(2,1)S(1)} async-done(((bf16[16,2,16,128]{3,2,1,0:T(8,128)(2,1)}), bf16[16,2,16,128]{3,2,1,0:T(8,128)(2,1)S(1)}, u32[]{:S(2)}, u32[]{:S(2)}) %all-to-all-start) | async-done | bytes 131104 | tf_op jit(solution)/shard_map/all_to_all | solution.py:436
  13.8 0.0 copy-done
  13.8 0.0 copy-done.1
  13.8 1.3 %arrivals.1 = bf16[6,2,32,128]{3,2,1,0:T(8,128)(2,1)} custom-call(bf16[16,2,16,128]{3,2,1,0:T(8,128)(2,1)S(1)} %all-to-all-done.got_ref, bf16[6,2,32,128]{3,2,1,0:T(8,128)(2,1)S(1)} %bitcast.42, bf16[48,128]{1,0:T(8,128)(2,1)S(1)} %bitcast.43), custom_call_target="tpu_custom_call" | custom-call | tf_op jit(solution)/shard_map/arrivals/pallas_call | solution.py:406
Async XLA Ops:
  2.4 11.5 %all-to-all-start = ((bf16[16,2,16,128]{3,2,1,0:T(8,128)(2,1)}), bf16[16,2,16,128]{3,2,1,0:T(8,128)(2,1)S(1)}, u32[]{:S(2)}, u32[]{:S(2)}) async-start(bf16[16,2,16,128]{3,2,1,0:T(8,128)(2,1)} %pack.1), calls=%async_computation | async-start | bytes 262144 | tf_op jit(solution)/shard_map/all_to_all | solution.py:436
  9.8 4.1 %copy-start = (bf16[6,2,4096]{2,1,0:T(2,128)(2,1)S(1)}, bf16[6,2,4096]{2,1,0:T(2,128)(2,1)}, u32[]{:S(2)}) copy-start(bf16[6,2,4096]{2,1,0:T(2,128)(2,1)} %param.20) | copy-start | bytes 294916
  9.8 4.0 %copy-start.1 = (bf16[6,2,2,256]{3,2,1,0:T(2,128)(2,1)S(1)}, bf16[6,2,2,256]{3,2,1,0:T(2,128)(2,1)}, u32[]{:S(2)}) copy-start(bf16[6,2,2,256]{3,2,1,0:T(2,128)(2,1)} %param.21) | copy-start | bytes 36868
where the time goes:
time: 15.4 us; the launch traced here: 15.1 us
  starting transfers between devices  7.42 us (48%)
  Pallas kernels  5.76 us (37%)
  waiting for transfers between devices  1.24 us (8%)
  between operations  0.66 us (4%)
    all_to_all x1, starting transfers between devices, shards(): lax.all_to_all(send, ('wide', 'tp'), split_axis=0, concat_axis=0, tiled=T...  7.42 us
    pallas_call x1, Pallas kernels, resident(): pl.pallas_call(resident_kernel, out_shape=jax.ShapeDtypeStruct(query.shap...  2.78 us
    pallas_call x1, Pallas kernels, pack(): pl.pallas_call(functools.partial(pack_kernel, tp, chips, KVH, 2 * block_t...  1.71 us
    pallas_call x1, Pallas kernels, arrivals(): pl.pallas_call(functools.partial(arrival_kernel, tp, groups, order, block...  1.26 us
    all_to_all x1, waiting for transfers between devices, shards(): lax.all_to_all(send, ('wide', 'tp'), split_axis=0, concat_axis=0, tiled=T...  1.24 us
  transfers between devices with their start and end apart: 1, of which 1 were waited for; matrix products, arithmetic and copies ran while one was open for 0% of the time, Pallas kernels for 18%

commit v1 on v0

--- a/solution.py
+++ b/solution.py
@@ -60,19 +60,18 @@
 
 
 def pack_kernel(
-    tp, chips, heads, block_rows, dest_hbm, blocks_hbm, codes_hbm, scales_hbm, send_hbm,
-    dest_ref, blocks_ref, codes_ref, scales_ref, empty_ref, values_ref, sems, out_sems,
+    tp, chips, heads, block_rows, dest_hbm, blocks_hbm, codes_hbm, scales_hbm, send_ref,
+    dest_ref, blocks_ref, codes_ref, scales_ref, sems,
 ):
     requests, all_rows = codes_ref.shape[:2]
     pairs = [
         (codes_hbm, codes_ref), (scales_hbm, scales_ref),
-        (dest_hbm, dest_ref), (blocks_hbm, blocks_ref), (empty_ref, send_hbm),
+        (dest_hbm, dest_ref), (blocks_hbm, blocks_ref),
     ]
     copies = [pltpu.make_async_copy(a, b, sems.at[i]) for i, (a, b) in enumerate(pairs)]
-    for copy in copies[:-1]:
+    for copy in copies:
         copy.start()
-    empty_ref[...] = jnp.full(empty_ref.shape, EMPTY, BF16)
-    copies[-1].start()
+    send_ref[...] = jnp.full(send_ref.shape, EMPTY, BF16)
     rows = all_rows // heads
     per_core = heads // tp
     row_block = over(iota((rows, HD), 0), block_rows)
@@ -83,36 +82,26 @@
     for copy in copies:
         copy.wait()
 
-    def hand_out(r):
+    def place(r):
         there = dest_ref[r]
         if chips is not None:
             there = functools.reduce(
                 jnp.add, [jnp.where(there == w, p, 0) for p, w in enumerate(chips)]
             )
-        target = send_hbm.at[pl.ds(there * tp, tp)]
-        return pltpu.make_async_copy(values_ref.at[r], target, out_sems.at[r])
-
-    def place(r):
+        last = there * tp + tp - 1
         held = row_block < blocks_ref[r]
         codes = dot_nn(by_head, codes_ref[r])
         scales = scales_ref[r].astype(F32)
         for j in range(heads):
             values = codes[j * rows : (j + 1) * rows] * scales[:, j : j + 1]
             values = jnp.where(held, values, EMPTY).astype(BF16)
-            values_ref[r, tp - 1 - j // per_core, j % per_core] = values
+            send_ref[last - j // per_core, j % per_core] = values
 
     if requests <= 8:
         for r in range(requests):
             place(r)
-        outs = [hand_out(r) for r in range(requests)]
-        for out in outs:
-            out.start()
-        for out in outs:
-            out.wait()
     else:
         pl.loop(0, requests)(place)
-        pl.loop(0, requests)(lambda r: hand_out(r).start())
-        pl.loop(0, requests)(lambda r: hand_out(r).wait())
 
 
 def resident_kernel(
@@ -235,7 +224,7 @@
 
 
 def arrival_kernel(
-    tp, groups, order, block_rows, got_ref, query_ref, new_ref, out_ref
+    tp, groups, order, block_rows, got_ref, query_ref, new_ref, out_hbm, out_ref, sems
 ):
     step = pl.program_id(0) if groups > 1 else 0
     chunks, heads, chunk_rows = got_ref.shape[:3]
@@ -247,8 +236,9 @@
     caches = [got_ref[:, h].reshape(columns, HD) for h in every]
     queries = [query_ref[:, h].reshape(rows, HD) for h in every]
     new = new_ref[...]
+    new_values = values_up(new)
     scores = [dot_nt(queries[h], caches[h]) for h in every]
-    new_all = dot_nt(jnp.concatenate(queries, axis=0), new)
+    new_all = [dot_nt(queries[h], new) for h in every]
     if order is None:
         slot_of = slots_by_matmul(got_ref, tp)
     else:
@@ -265,28 +255,27 @@
     )
     new_head = jnp.where(new_here, mod(over(new_col, 2), heads), heads)
 
-    scores = [
-        jnp.concatenate(
+    copies = []
+    for h in every:
+        score = jnp.concatenate(
             [
                 jnp.where(mine[a], scores[h][a * per_head : (a + 1) * per_head] * SCORE_SCALE, NEGATIVE)
                 for a in range(slots)
             ],
             axis=0,
         )
-        for h in every
-    ]
-    new_scores = [
-        jnp.where(new_head == h, new_all[h * rows : (h + 1) * rows] * SCORE_SCALE, NEGATIVE)
-        for h in every
-    ]
-    top = [top_of(scores[h], new_scores[h]) for h in every]
-    weights = [jnp.exp(scores[h] - top[h]) for h in every]
-    new_weights = [jnp.exp(new_scores[h] - top[h]) for h in every]
-    total = [sum_of(weights[h], new_weights[h]) for h in every]
-    new_mixed = dot_nn(jnp.concatenate(new_weights, axis=0).astype(BF16), values_up(new))
-    for h in every:
-        mixed = dot_nn(to_values(weights[h]), caches[h]) + new_mixed[h * rows : (h + 1) * rows]
-        out_ref[:, h] = (mixed * (1.0 / total[h])).astype(BF16).reshape(slots, per_head, HD)
+        new_score = jnp.where(new_head == h, new_all[h] * SCORE_SCALE, NEGATIVE)
+        top = top_of(score, new_score)
+        weights = jnp.exp(score - top)
+        new_weights = jnp.exp(new_score - top)
+        total = sum_of(weights, new_weights)
+        mixed = dot_nn(to_values(weights), caches[h]) + dot_nn(new_weights.astype(BF16), new_values)
+        out_ref[h] = (mixed * (1.0 / total)).astype(BF16).reshape(slots, per_head, HD)
+        target = out_hbm.at[pl.ds(step * slots, slots), h]
+        copies.append(pltpu.make_async_copy(out_ref.at[h], target, sems.at[h]))
+        copies[-1].start()
+    for copy in copies:
+        copy.wait()
 
 
 def whole(memory_space=pltpu.VMEM):
@@ -316,16 +305,13 @@
         functools.partial(pack_kernel, tp, chips, KVH, 2 * block_tokens),
         out_shape=jax.ShapeDtypeStruct((peers * tp,) + chunk, BF16),
         in_specs=[whole(pltpu.HBM)] * len(ins),
-        out_specs=whole(pltpu.HBM),
+        out_specs=whole(),
         scratch_shapes=[
             pltpu.SMEM(req_dest.shape, jnp.int32),
             pltpu.SMEM(req_blocks.shape, jnp.int32),
             pltpu.VMEM(codes.shape, BF16),
             pltpu.VMEM(scales.shape, BF16),
-            pltpu.VMEM((peers * tp,) + chunk, BF16),
-            pltpu.VMEM((requests, tp) + chunk, BF16),
-            pltpu.SemaphoreType.DMA((5,)),
-            pltpu.SemaphoreType.DMA((requests,)),
+            pltpu.SemaphoreType.DMA((len(ins),)),
         ],
         compiler_params=limit(24),
         name="pack",
@@ -408,7 +394,11 @@
         out_shape=jax.ShapeDtypeStruct(query.shape, BF16),
         grid=(groups,) if groups > 1 else (),
         in_specs=[whole(), part(query, size), part(new, new.shape[0] // groups)],
-        out_specs=part(query, size),
+        out_specs=whole(pltpu.HBM),
+        scratch_shapes=[
+            pltpu.VMEM((heads, size) + query.shape[2:], BF16),
+            pltpu.SemaphoreType.DMA((heads,)),
+        ],
         compiler_params=limit(16 if small else 48),
         name="arrivals",
     )(got, query, new)

time: 15.4 us -> 15.4 us (level)
  no operation moved by 1% of the time
where the time goes in v1:
time: 15.4 us; the launch traced here: 15.1 us
  starting transfers between devices  7.42 us (48%)
  Pallas kernels  5.78 us (38%)
  waiting for transfers between devices  1.24 us (8%)
  between operations  0.66 us (4%)
    all_to_all x1, starting transfers between devices, shards(): lax.all_to_all(send, ('wide', 'tp'), split_axis=0, concat_axis=0, tiled=T...  7.42 us
    pallas_call x1, Pallas kernels, resident(): pl.pallas_call(resident_kernel, out_shape=jax.ShapeDtypeStruct(query.shap...  2.78 us
    pallas_call x1, Pallas kernels, pack(): pl.pallas_call(functools.partial(pack_kernel, tp, chips, KVH, 2 * block_t...  1.69 us
    pallas_call x1, Pallas kernels, arrivals(): pl.pallas_call(functools.partial(arrival_kernel, tp, groups, order, block...  1.31 us
    all_to_all x1, waiting for transfers between devices, shards(): lax.all_to_all(send, ('wide', 'tp'), split_axis=0, concat_axis=0, tiled=T...  1.24 us
  transfers between devices with their start and end apart: 1, of which 1 were waited for; matrix products, arithmetic and copies ran while one was open for 0% of the time, Pallas kernels for 18%

profile of v1, /device:TPU:1, one launch (start us, length us, event | category | flops | bytes accessed | tf_op | source)
XLA Modules:
  0.0 15.1 jit_solution(6002487630873717932)
XLA Ops:
  0.6 1.7 %pack.1 = bf16[16,2,16,128]{3,2,1,0:T(8,128)(2,1)} custom-call(s32[4]{0:T(128)} %dest_hbm.1, s32[4]{0:T(128)} %blocks_hbm.1, bf16[4,64,128]{2,1,0:T(8,128)(2,1)} %bitcast.48, bf16[4,16,4]{2,1,0:T(8,128)(2,1)} %bitcast.50), custom_call_target="tpu_custom_call" | custom-call | tf_op jit(solution)/shard_map/pack/pallas_call | solution.py:304
  2.3 7.4 %all-to-all-start = ((bf16[16,2,16,128]{3,2,1,0:T(8,128)(2,1)}), bf16[16,2,16,128]{3,2,1,0:T(8,128)(2,1)S(1)}, u32[]{:S(2)}, u32[]{:S(2)}) async-start(bf16[16,2,16,128]{3,2,1,0:T(8,128)(2,1)} %pack.1), calls=%async_computation | async-start | bytes 262144 | tf_op jit(solution)/shard_map/all_to_all | solution.py:426
  9.8 0.0 copy-start
  9.8 0.0 copy-start.1
  9.8 2.8 %resident.1 = bf16[8,64,128]{2,1,0:T(8,128)(2,1)} custom-call(s32[8]{0:T(128)} %len_hbm.1, bf16[8,256,128]{2,1,0:T(8,128)(2,1)} %bitcast.44, bf16[8,2,2,64]{3,2,1,0:T(2,128)(2,1)} %bitcast.51, bf16[8,64,128]{2,1,0:T(8,128)(2,1)} %bitcast.45, bf16[64,128]{1,0:T(8,128)(2,1)} %bitcast.49), custom_call_target="tpu_custom_call" | custom-call | flops 67108864 | bytes 786432 | tf_op jit(solution)/shard_map/resident/pallas_call | solution.py:358
  12.6 1.2 %all-to-all-done.got_ref = bf16[16,2,16,128]{3,2,1,0:T(8,128)(2,1)S(1)} async-done(((bf16[16,2,16,128]{3,2,1,0:T(8,128)(2,1)}), bf16[16,2,16,128]{3,2,1,0:T(8,128)(2,1)S(1)}, u32[]{:S(2)}, u32[]{:S(2)}) %all-to-all-start) | async-done | bytes 131104 | tf_op jit(solution)/shard_map/all_to_all | solution.py:426
  13.8 0.0 copy-done
  13.8 0.0 copy-done.1
  13.8 1.3 %arrivals.1 = bf16[6,2,32,128]{3,2,1,0:T(8,128)(2,1)} custom-call(bf16[16,2,16,128]{3,2,1,0:T(8,128)(2,1)S(1)} %all-to-all-done.got_ref, bf16[6,2,32,128]{3,2,1,0:T(8,128)(2,1)S(1)} %bitcast.42, bf16[48,128]{1,0:T(8,128)(2,1)S(1)} %bitcast.43), custom_call_target="tpu_custom_call" | custom-call | tf_op jit(solution)/shard_map/arrivals/pallas_call | solution.py:392
Async XLA Ops:
  2.3 11.5 %all-to-all-start = ((bf16[16,2,16,128]{3,2,1,0:T(8,128)(2,1)}), bf16[16,2,16,128]{3,2,1,0:T(8,128)(2,1)S(1)}, u32[]{:S(2)}, u32[]{:S(2)}) async-start(bf16[16,2,16,128]{3,2,1,0:T(8,128)(2,1)} %pack.1), calls=%async_computation | async-start | bytes 262144 | tf_op jit(solution)/shard_map/all_to_all | solution.py:426
  9.8 4.1 %copy-start = (bf16[6,2,4096]{2,1,0:T(2,128)(2,1)S(1)}, bf16[6,2,4096]{2,1,0:T(2,128)(2,1)}, u32[]{:S(2)}) copy-start(bf16[6,2,4096]{2,1,0:T(2,128)(2,1)} %param.20) | copy-start | bytes 294916
  9.8 4.0 %copy-start.1 = (bf16[6,2,2,256]{3,2,1,0:T(2,128)(2,1)S(1)}, bf16[6,2,2,256]{3,2,1,0:T(2,128)(2,1)}, u32[]{:S(2)}) copy-start(bf16[6,2,2,256]{3,2,1,0:T(2,128)(2,1)} %param.21) | copy-start | bytes 36868

commit v2 on v0

--- a/solution.py
+++ b/solution.py
@@ -60,19 +60,18 @@
 
 
 def pack_kernel(
-    tp, chips, heads, block_rows, dest_hbm, blocks_hbm, codes_hbm, scales_hbm, send_hbm,
-    dest_ref, blocks_ref, codes_ref, scales_ref, empty_ref, values_ref, sems, out_sems,
+    tp, order, heads, block_rows, dest_hbm, blocks_hbm, codes_hbm, scales_hbm, send_ref,
+    dest_ref, blocks_ref, codes_ref, scales_ref, sems,
 ):
     requests, all_rows = codes_ref.shape[:2]
     pairs = [
         (codes_hbm, codes_ref), (scales_hbm, scales_ref),
-        (dest_hbm, dest_ref), (blocks_hbm, blocks_ref), (empty_ref, send_hbm),
+        (dest_hbm, dest_ref), (blocks_hbm, blocks_ref),
     ]
     copies = [pltpu.make_async_copy(a, b, sems.at[i]) for i, (a, b) in enumerate(pairs)]
-    for copy in copies[:-1]:
+    for copy in copies:
         copy.start()
-    empty_ref[...] = jnp.full(empty_ref.shape, EMPTY, BF16)
-    copies[-1].start()
+    send_ref[...] = jnp.full(send_ref.shape, EMPTY, BF16)
     rows = all_rows // heads
     per_core = heads // tp
     row_block = over(iota((rows, HD), 0), block_rows)
@@ -83,36 +82,28 @@
     for copy in copies:
         copy.wait()
 
-    def hand_out(r):
+    def place(r):
         there = dest_ref[r]
-        if chips is not None:
-            there = functools.reduce(
-                jnp.add, [jnp.where(there == w, p, 0) for p, w in enumerate(chips)]
-            )
-        target = send_hbm.at[pl.ds(there * tp, tp)]
-        return pltpu.make_async_copy(values_ref.at[r], target, out_sems.at[r])
-
-    def place(r):
+        spots = [there * tp + t for t in range(tp)]
+        if order is not None:
+            for t in range(tp):
+                at = {core // tp: p for p, core in enumerate(order) if core % tp == t}
+                spots[t] = functools.reduce(
+                    jnp.add, [jnp.where(there == w, p, 0) for w, p in at.items()]
+                )
         held = row_block < blocks_ref[r]
         codes = dot_nn(by_head, codes_ref[r])
         scales = scales_ref[r].astype(F32)
         for j in range(heads):
             values = codes[j * rows : (j + 1) * rows] * scales[:, j : j + 1]
             values = jnp.where(held, values, EMPTY).astype(BF16)
-            values_ref[r, tp - 1 - j // per_core, j % per_core] = values
+            send_ref[spots[j // per_core], j % per_core] = values
 
     if requests <= 8:
         for r in range(requests):
             place(r)
-        outs = [hand_out(r) for r in range(requests)]
-        for out in outs:
-            out.start()
-        for out in outs:
-            out.wait()
     else:
         pl.loop(0, requests)(place)
-        pl.loop(0, requests)(lambda r: hand_out(r).start())
-        pl.loop(0, requests)(lambda r: hand_out(r).wait())
 
 
 def resident_kernel(
@@ -301,7 +292,7 @@
     return pltpu.CompilerParams(vmem_limit_bytes=mib * 2**20)
 
 
-def pack(pre_codes, pre_scales, req_dest, req_blocks, peers, tp, chips):
+def pack(pre_codes, pre_scales, req_dest, req_blocks, peers, tp, order):
     requests, blocks, block_tokens = pre_codes.shape[:3]
     tokens = blocks * block_tokens
     codes = (
@@ -313,19 +304,16 @@
     ins = [req_dest, req_blocks, codes, scales]
     chunk = (KVH // tp, tokens * 2, HD)
     return pl.pallas_call(
-        functools.partial(pack_kernel, tp, chips, KVH, 2 * block_tokens),
+        functools.partial(pack_kernel, tp, order, KVH, 2 * block_tokens),
         out_shape=jax.ShapeDtypeStruct((peers * tp,) + chunk, BF16),
         in_specs=[whole(pltpu.HBM)] * len(ins),
-        out_specs=whole(pltpu.HBM),
+        out_specs=whole(),
         scratch_shapes=[
             pltpu.SMEM(req_dest.shape, jnp.int32),
             pltpu.SMEM(req_blocks.shape, jnp.int32),
             pltpu.VMEM(codes.shape, BF16),
             pltpu.VMEM(scales.shape, BF16),
-            pltpu.VMEM((peers * tp,) + chunk, BF16),
-            pltpu.VMEM((requests, tp) + chunk, BF16),
-            pltpu.SemaphoreType.DMA((5,)),
-            pltpu.SemaphoreType.DMA((requests,)),
+            pltpu.SemaphoreType.DMA((len(ins),)),
         ],
         compiler_params=limit(24),
         name="pack",
@@ -429,17 +417,17 @@
 ):
     peers = lax.axis_size("wide")
     tp = lax.axis_size("tp")
-    chips = [5, 6, 7, 1, 0, 2, 3, 4] if peers == 8 else None
-    cores = [w * tp + t for w in chips or range(peers) for t in reversed(range(tp))]
-    order = chips and cores
-    send = pack(pre_codes, pre_scales, req_dest, req_blocks, peers, tp, chips)
+    order = None
+    if peers * tp == 16:
+        order = [11, 13, 15, 3, 1, 5, 7, 9, 10, 12, 14, 2, 0, 4, 6, 8]
+    send = pack(pre_codes, pre_scales, req_dest, req_blocks, peers, tp, order)
     got = lax.all_to_all(
         send,
         ("wide", "tp"),
         split_axis=0,
         concat_axis=0,
         tiled=True,
-        axis_index_groups=[cores],
+        axis_index_groups=[order or list(range(peers * tp))],
     )
     res_out = resident(cache_rows(res_codes), res_scales, res_len, res_query, res_new)
     block_rows = 2 * pre_codes.shape[2]

time: 15.4 us -> 16.3 us (1.058)
  the two profiles are of different devices: /device:TPU:1 before, /device:TPU:0 now
where the time goes in v2:
time: 16.3 us; the launch traced here: 16.1 us
  starting transfers between devices  7.79 us (48%)
  Pallas kernels  5.73 us (35%)
  waiting for transfers between devices  1.86 us (11%)
  between operations  0.66 us (4%)
    all_to_all x1, starting transfers between devices, shards(): lax.all_to_all(send, ('wide', 'tp'), split_axis=0, concat_axis=0, tiled=T...  7.79 us
    pallas_call x1, Pallas kernels, resident(): pl.pallas_call(resident_kernel, out_shape=jax.ShapeDtypeStruct(query.shap...  2.78 us
    all_to_all x1, waiting for transfers between devices, shards(): lax.all_to_all(send, ('wide', 'tp'), split_axis=0, concat_axis=0, tiled=T...  1.86 us
    pallas_call x1, Pallas kernels, pack(): pl.pallas_call(functools.partial(pack_kernel, tp, order, KVH, 2 * block_t...  1.69 us
    pallas_call x1, Pallas kernels, arrivals(): pl.pallas_call(functools.partial(arrival_kernel, tp, groups, order, block...  1.27 us
  transfers between devices with their start and end apart: 1, of which 1 were waited for; matrix products, arithmetic and copies ran while one was open for 0% of the time, Pallas kernels for 17%

profile of v2, /device:TPU:0, one launch (start us, length us, event | category | flops | bytes accessed | tf_op | source)
XLA Modules:
  0.0 16.1 jit_solution(12034717062279523902)
XLA Ops:
  0.6 1.7 %pack.1 = bf16[16,2,16,128]{3,2,1,0:T(8,128)(2,1)} custom-call(s32[4]{0:T(128)} %dest_hbm.1, s32[4]{0:T(128)} %blocks_hbm.1, bf16[4,64,128]{2,1,0:T(8,128)(2,1)} %bitcast.48, bf16[4,16,4]{2,1,0:T(8,128)(2,1)} %bitcast.50), custom_call_target="tpu_custom_call" | custom-call | tf_op jit(solution)/shard_map/pack/pallas_call | solution.py:306
  2.3 7.8 %all-to-all-start = ((bf16[16,2,16,128]{3,2,1,0:T(8,128)(2,1)}), bf16[16,2,16,128]{3,2,1,0:T(8,128)(2,1)S(1)}, u32[]{:S(2)}, u32[]{:S(2)}) async-start(bf16[16,2,16,128]{3,2,1,0:T(8,128)(2,1)} %pack.1), calls=%async_computation | async-start | bytes 262144 | tf_op jit(solution)/shard_map/all_to_all | solution.py:424
  10.1 0.0 copy-start
  10.1 0.0 copy-start.1
  10.1 2.8 %resident.1 = bf16[8,64,128]{2,1,0:T(8,128)(2,1)} custom-call(s32[8]{0:T(128)} %len_hbm.1, bf16[8,256,128]{2,1,0:T(8,128)(2,1)} %bitcast.44, bf16[8,2,2,64]{3,2,1,0:T(2,128)(2,1)} %bitcast.51, bf16[8,64,128]{2,1,0:T(8,128)(2,1)} %bitcast.45, bf16[64,128]{1,0:T(8,128)(2,1)} %bitcast.49), custom_call_target="tpu_custom_call" | custom-call | flops 67108864 | bytes 786432 | tf_op jit(solution)/shard_map/resident/pallas_call | solution.py:360
  12.9 1.9 %all-to-all-done.got_ref = bf16[16,2,16,128]{3,2,1,0:T(8,128)(2,1)S(1)} async-done(((bf16[16,2,16,128]{3,2,1,0:T(8,128)(2,1)}), bf16[16,2,16,128]{3,2,1,0:T(8,128)(2,1)S(1)}, u32[]{:S(2)}, u32[]{:S(2)}) %all-to-all-start) | async-done | bytes 131104 | tf_op jit(solution)/shard_map/all_to_all | solution.py:424
  14.8 0.0 copy-done
  14.8 0.0 copy-done.1
  14.8 1.3 %arrivals.1 = bf16[6,2,32,128]{3,2,1,0:T(8,128)(2,1)} custom-call(bf16[16,2,16,128]{3,2,1,0:T(8,128)(2,1)S(1)} %all-to-all-done.got_ref, bf16[6,2,32,128]{3,2,1,0:T(8,128)(2,1)S(1)} %bitcast.42, bf16[48,128]{1,0:T(8,128)(2,1)S(1)} %bitcast.43), custom_call_target="tpu_custom_call" | custom-call | tf_op jit(solution)/shard_map/arrivals/pallas_call | solution.py:394
Async XLA Ops:
  2.3 12.5 %all-to-all-start = ((bf16[16,2,16,128]{3,2,1,0:T(8,128)(2,1)}), bf16[16,2,16,128]{3,2,1,0:T(8,128)(2,1)S(1)}, u32[]{:S(2)}, u32[]{:S(2)}) async-start(bf16[16,2,16,128]{3,2,1,0:T(8,128)(2,1)} %pack.1), calls=%async_computation | async-start | bytes 262144 | tf_op jit(solution)/shard_map/all_to_all | solution.py:424
  10.1 4.7 %copy-start = (bf16[6,2,4096]{2,1,0:T(2,128)(2,1)S(1)}, bf16[6,2,4096]{2,1,0:T(2,128)(2,1)}, u32[]{:S(2)}) copy-start(bf16[6,2,4096]{2,1,0:T(2,128)(2,1)} %param.20) | copy-start | bytes 294916
  10.1 4.7 %copy-start.1 = (bf16[6,2,2,256]{3,2,1,0:T(2,128)(2,1)S(1)}, bf16[6,2,2,256]{3,2,1,0:T(2,128)(2,1)}, u32[]{:S(2)}) copy-start(bf16[6,2,2,256]{3,2,1,0:T(2,128)(2,1)} %param.21) | copy-start | bytes 36868

commit v3 on v2

--- a/solution.py
+++ b/solution.py
@@ -419,7 +419,7 @@
     tp = lax.axis_size("tp")
     order = None
     if peers * tp == 16:
-        order = [11, 13, 15, 3, 1, 5, 7, 9, 10, 12, 14, 2, 0, 4, 6, 8]
+        order = [10, 11, 12, 13, 14, 15, 3, 2, 1, 0, 4, 5, 6, 7, 8, 9]
     send = pack(pre_codes, pre_scales, req_dest, req_blocks, peers, tp, order)
     got = lax.all_to_all(
         send,

time: 16.3 us -> 16.6 us (1.018)
  starting transfers between devices: 7.79 us -> 8.35 us
  waiting for transfers between devices: 1.86 us -> 1.54 us
    all_to_all x1, starting transfers between devices: 7.79 us -> 8.35 us  [shards(): lax.all_to_all(send, ('wide', 'tp'), split_axis=0, concat_axis=0, tiled=T...]
    all_to_all x1, waiting for transfers between devices: 1.86 us -> 1.54 us  [shards(): lax.all_to_all(send, ('wide', 'tp'), split_axis=0, concat_axis=0, tiled=T...]
where the time goes in v3:
time: 16.6 us; the launch traced here: 16.3 us
  starting transfers between devices  8.35 us (50%)
  Pallas kernels  5.73 us (35%)
  waiting for transfers between devices  1.54 us (9%)
  between operations  0.66 us (4%)
    all_to_all x1, starting transfers between devices, shards(): lax.all_to_all(send, ('wide', 'tp'), split_axis=0, concat_axis=0, tiled=T...  8.35 us
    pallas_call x1, Pallas kernels, resident(): pl.pallas_call(resident_kernel, out_shape=jax.ShapeDtypeStruct(query.shap...  2.78 us
    pallas_call x1, Pallas kernels, pack(): pl.pallas_call(functools.partial(pack_kernel, tp, order, KVH, 2 * block_t...  1.69 us
    all_to_all x1, waiting for transfers between devices, shards(): lax.all_to_all(send, ('wide', 'tp'), split_axis=0, concat_axis=0, tiled=T...  1.54 us
    pallas_call x1, Pallas kernels, arrivals(): pl.pallas_call(functools.partial(arrival_kernel, tp, groups, order, block...  1.26 us
  transfers between devices with their start and end apart: 1, of which 1 were waited for; matrix products, arithmetic and copies ran while one was open for 0% of the time, Pallas kernels for 17%

profile of v3, /device:TPU:0, one launch (start us, length us, event | category | flops | bytes accessed | tf_op | source)
XLA Modules:
  0.0 16.3 jit_solution(1954318838336539844)
XLA Ops:
  0.6 1.7 %pack.1 = bf16[16,2,16,128]{3,2,1,0:T(8,128)(2,1)} custom-call(s32[4]{0:T(128)} %dest_hbm.1, s32[4]{0:T(128)} %blocks_hbm.1, bf16[4,64,128]{2,1,0:T(8,128)(2,1)} %bitcast.48, bf16[4,16,4]{2,1,0:T(8,128)(2,1)} %bitcast.50), custom_call_target="tpu_custom_call" | custom-call | tf_op jit(solution)/shard_map/pack/pallas_call | solution.py:306
  2.3 8.4 %all-to-all-start = ((bf16[16,2,16,128]{3,2,1,0:T(8,128)(2,1)}), bf16[16,2,16,128]{3,2,1,0:T(8,128)(2,1)S(1)}, u32[]{:S(2)}, u32[]{:S(2)}) async-start(bf16[16,2,16,128]{3,2,1,0:T(8,128)(2,1)} %pack.1), calls=%async_computation | async-start | bytes 262144 | tf_op jit(solution)/shard_map/all_to_all | solution.py:424
  10.7 0.0 copy-start
  10.7 0.0 copy-start.1
  10.7 2.8 %resident.1 = bf16[8,64,128]{2,1,0:T(8,128)(2,1)} custom-call(s32[8]{0:T(128)} %len_hbm.1, bf16[8,256,128]{2,1,0:T(8,128)(2,1)} %bitcast.44, bf16[8,2,2,64]{3,2,1,0:T(2,128)(2,1)} %bitcast.51, bf16[8,64,128]{2,1,0:T(8,128)(2,1)} %bitcast.45, bf16[64,128]{1,0:T(8,128)(2,1)} %bitcast.49), custom_call_target="tpu_custom_call" | custom-call | flops 67108864 | bytes 786432 | tf_op jit(solution)/shard_map/resident/pallas_call | solution.py:360
  13.5 1.5 %all-to-all-done.got_ref = bf16[16,2,16,128]{3,2,1,0:T(8,128)(2,1)S(1)} async-done(((bf16[16,2,16,128]{3,2,1,0:T(8,128)(2,1)}), bf16[16,2,16,128]{3,2,1,0:T(8,128)(2,1)S(1)}, u32[]{:S(2)}, u32[]{:S(2)}) %all-to-all-start) | async-done | bytes 131104 | tf_op jit(solution)/shard_map/all_to_all | solution.py:424
  15.0 0.0 copy-done
  15.0 0.0 copy-done.1
  15.0 1.3 %arrivals.1 = bf16[6,2,32,128]{3,2,1,0:T(8,128)(2,1)} custom-call(bf16[16,2,16,128]{3,2,1,0:T(8,128)(2,1)S(1)} %all-to-all-done.got_ref, bf16[6,2,32,128]{3,2,1,0:T(8,128)(2,1)S(1)} %bitcast.42, bf16[48,128]{1,0:T(8,128)(2,1)S(1)} %bitcast.43), custom_call_target="tpu_custom_call" | custom-call | tf_op jit(solution)/shard_map/arrivals/pallas_call | solution.py:394
Async XLA Ops:
  2.3 12.7 %all-to-all-start = ((bf16[16,2,16,128]{3,2,1,0:T(8,128)(2,1)}), bf16[16,2,16,128]{3,2,1,0:T(8,128)(2,1)S(1)}, u32[]{:S(2)}, u32[]{:S(2)}) async-start(bf16[16,2,16,128]{3,2,1,0:T(8,128)(2,1)} %pack.1), calls=%async_computation | async-start | bytes 262144 | tf_op jit(solution)/shard_map/all_to_all | solution.py:424
  10.7 4.3 %copy-start = (bf16[6,2,4096]{2,1,0:T(2,128)(2,1)S(1)}, bf16[6,2,4096]{2,1,0:T(2,128)(2,1)}, u32[]{:S(2)}) copy-start(bf16[6,2,4096]{2,1,0:T(2,128)(2,1)} %param.20) | copy-start | bytes 294916
  10.7 4.3 %copy-start.1 = (bf16[6,2,2,256]{3,2,1,0:T(2,128)(2,1)S(1)}, bf16[6,2,2,256]{3,2,1,0:T(2,128)(2,1)}, u32[]{:S(2)}) copy-start(bf16[6,2,2,256]{3,2,1,0:T(2,128)(2,1)} %param.21) | copy-start | bytes 36868

commit v4 on v3

--- a/solution.py
+++ b/solution.py
@@ -419,7 +419,7 @@
     tp = lax.axis_size("tp")
     order = None
     if peers * tp == 16:
-        order = [10, 11, 12, 13, 14, 15, 3, 2, 1, 0, 4, 5, 6, 7, 8, 9]
+        order = [11, 10, 13, 12, 15, 14, 3, 2, 1, 0, 4, 5, 6, 7, 9, 8]
     send = pack(pre_codes, pre_scales, req_dest, req_blocks, peers, tp, order)
     got = lax.all_to_all(
         send,

time: 16.6 us -> 15.3 us (0.922)
  the two profiles are of different devices: /device:TPU:0 before, /device:TPU:1 now
where the time goes in v4:
time: 15.3 us; the launch traced here: 15.1 us
  starting transfers between devices  7.42 us (48%)
  Pallas kernels  5.73 us (37%)
  waiting for transfers between devices  1.24 us (8%)
  between operations  0.66 us (4%)
    all_to_all x1, starting transfers between devices, shards(): lax.all_to_all(send, ('wide', 'tp'), split_axis=0, concat_axis=0, tiled=T...  7.42 us
    pallas_call x1, Pallas kernels, resident(): pl.pallas_call(resident_kernel, out_shape=jax.ShapeDtypeStruct(query.shap...  2.78 us
    pallas_call x1, Pallas kernels, pack(): pl.pallas_call(functools.partial(pack_kernel, tp, order, KVH, 2 * block_t...  1.69 us
    pallas_call x1, Pallas kernels, arrivals(): pl.pallas_call(functools.partial(arrival_kernel, tp, groups, order, block...  1.27 us
    all_to_all x1, waiting for transfers between devices, shards(): lax.all_to_all(send, ('wide', 'tp'), split_axis=0, concat_axis=0, tiled=T...  1.24 us
  transfers between devices with their start and end apart: 1, of which 1 were waited for; matrix products, arithmetic and copies ran while one was open for 0% of the time, Pallas kernels for 18%

profile of v4, /device:TPU:1, one launch (start us, length us, event | category | flops | bytes accessed | tf_op | source)
XLA Modules:
  0.0 15.1 jit_solution(7714735451974270523)
XLA Ops:
  0.6 1.7 %pack.1 = bf16[16,2,16,128]{3,2,1,0:T(8,128)(2,1)} custom-call(s32[4]{0:T(128)} %dest_hbm.1, s32[4]{0:T(128)} %blocks_hbm.1, bf16[4,64,128]{2,1,0:T(8,128)(2,1)} %bitcast.48, bf16[4,16,4]{2,1,0:T(8,128)(2,1)} %bitcast.50), custom_call_target="tpu_custom_call" | custom-call | tf_op jit(solution)/shard_map/pack/pallas_call | solution.py:306
  2.3 7.4 %all-to-all-start = ((bf16[16,2,16,128]{3,2,1,0:T(8,128)(2,1)}), bf16[16,2,16,128]{3,2,1,0:T(8,128)(2,1)S(1)}, u32[]{:S(2)}, u32[]{:S(2)}) async-start(bf16[16,2,16,128]{3,2,1,0:T(8,128)(2,1)} %pack.1), calls=%async_computation | async-start | bytes 262144 | tf_op jit(solution)/shard_map/all_to_all | solution.py:424
  9.8 0.0 copy-start
  9.8 0.0 copy-start.1
  9.8 2.8 %resident.1 = bf16[8,64,128]{2,1,0:T(8,128)(2,1)} custom-call(s32[8]{0:T(128)} %len_hbm.1, bf16[8,256,128]{2,1,0:T(8,128)(2,1)} %bitcast.44, bf16[8,2,2,64]{3,2,1,0:T(2,128)(2,1)} %bitcast.51, bf16[8,64,128]{2,1,0:T(8,128)(2,1)} %bitcast.45, bf16[64,128]{1,0:T(8,128)(2,1)} %bitcast.49), custom_call_target="tpu_custom_call" | custom-call | flops 67108864 | bytes 786432 | tf_op jit(solution)/shard_map/resident/pallas_call | solution.py:360
  12.6 1.2 %all-to-all-done.got_ref = bf16[16,2,16,128]{3,2,1,0:T(8,128)(2,1)S(1)} async-done(((bf16[16,2,16,128]{3,2,1,0:T(8,128)(2,1)}), bf16[16,2,16,128]{3,2,1,0:T(8,128)(2,1)S(1)}, u32[]{:S(2)}, u32[]{:S(2)}) %all-to-all-start) | async-done | bytes 131104 | tf_op jit(solution)/shard_map/all_to_all | solution.py:424
  13.8 0.0 copy-done
  13.8 0.0 copy-done.1
  13.8 1.3 %arrivals.1 = bf16[6,2,32,128]{3,2,1,0:T(8,128)(2,1)} custom-call(bf16[16,2,16,128]{3,2,1,0:T(8,128)(2,1)S(1)} %all-to-all-done.got_ref, bf16[6,2,32,128]{3,2,1,0:T(8,128)(2,1)S(1)} %bitcast.42, bf16[48,128]{1,0:T(8,128)(2,1)S(1)} %bitcast.43), custom_call_target="tpu_custom_call" | custom-call | tf_op jit(solution)/shard_map/arrivals/pallas_call | solution.py:394
Async XLA Ops:
  2.3 11.5 %all-to-all-start = ((bf16[16,2,16,128]{3,2,1,0:T(8,128)(2,1)}), bf16[16,2,16,128]{3,2,1,0:T(8,128)(2,1)S(1)}, u32[]{:S(2)}, u32[]{:S(2)}) async-start(bf16[16,2,16,128]{3,2,1,0:T(8,128)(2,1)} %pack.1), calls=%async_computation | async-start | bytes 262144 | tf_op jit(solution)/shard_map/all_to_all | solution.py:424
  9.8 4.1 %copy-start = (bf16[6,2,4096]{2,1,0:T(2,128)(2,1)S(1)}, bf16[6,2,4096]{2,1,0:T(2,128)(2,1)}, u32[]{:S(2)}) copy-start(bf16[6,2,4096]{2,1,0:T(2,128)(2,1)} %param.20) | copy-start | bytes 294916
  9.8 4.0 %copy-start.1 = (bf16[6,2,2,256]{3,2,1,0:T(2,128)(2,1)S(1)}, bf16[6,2,2,256]{3,2,1,0:T(2,128)(2,1)}, u32[]{:S(2)}) copy-start(bf16[6,2,2,256]{3,2,1,0:T(2,128)(2,1)} %param.21) | copy-start | bytes 36868

commit v5 on v4

--- a/solution.py
+++ b/solution.py
@@ -419,7 +419,7 @@
     tp = lax.axis_size("tp")
     order = None
     if peers * tp == 16:
-        order = [11, 10, 13, 12, 15, 14, 3, 2, 1, 0, 4, 5, 6, 7, 9, 8]
+        order = [11, 10, 12, 13, 14, 15, 3, 2, 1, 0, 5, 4, 7, 6, 9, 8]
     send = pack(pre_codes, pre_scales, req_dest, req_blocks, peers, tp, order)
     got = lax.all_to_all(
         send,

time: 15.3 us -> 16 us (1.046)
  the two profiles are of different devices: /device:TPU:1 before, /device:TPU:0 now
where the time goes in v5:
time: 16 us; the launch traced here: 15.7 us
  starting transfers between devices  7.79 us (49%)
  Pallas kernels  5.73 us (36%)
  waiting for transfers between devices  1.54 us (10%)
  between operations  0.66 us (4%)
    all_to_all x1, starting transfers between devices, shards(): lax.all_to_all(send, ('wide', 'tp'), split_axis=0, concat_axis=0, tiled=T...  7.79 us
    pallas_call x1, Pallas kernels, resident(): pl.pallas_call(resident_kernel, out_shape=jax.ShapeDtypeStruct(query.shap...  2.78 us
    pallas_call x1, Pallas kernels, pack(): pl.pallas_call(functools.partial(pack_kernel, tp, order, KVH, 2 * block_t...  1.69 us
    all_to_all x1, waiting for transfers between devices, shards(): lax.all_to_all(send, ('wide', 'tp'), split_axis=0, concat_axis=0, tiled=T...  1.54 us
    pallas_call x1, Pallas kernels, arrivals(): pl.pallas_call(functools.partial(arrival_kernel, tp, groups, order, block...  1.26 us
  transfers between devices with their start and end apart: 1, of which 1 were waited for; matrix products, arithmetic and copies ran while one was open for 0% of the time, Pallas kernels for 18%

profile of v5, /device:TPU:0, one launch (start us, length us, event | category | flops | bytes accessed | tf_op | source)
XLA Modules:
  0.0 15.7 jit_solution(14479696162253421716)
XLA Ops:
  0.6 1.7 %pack.1 = bf16[16,2,16,128]{3,2,1,0:T(8,128)(2,1)} custom-call(s32[4]{0:T(128)} %dest_hbm.1, s32[4]{0:T(128)} %blocks_hbm.1, bf16[4,64,128]{2,1,0:T(8,128)(2,1)} %bitcast.48, bf16[4,16,4]{2,1,0:T(8,128)(2,1)} %bitcast.50), custom_call_target="tpu_custom_call" | custom-call | tf_op jit(solution)/shard_map/pack/pallas_call | solution.py:306
  2.3 7.8 %all-to-all-start = ((bf16[16,2,16,128]{3,2,1,0:T(8,128)(2,1)}), bf16[16,2,16,128]{3,2,1,0:T(8,128)(2,1)S(1)}, u32[]{:S(2)}, u32[]{:S(2)}) async-start(bf16[16,2,16,128]{3,2,1,0:T(8,128)(2,1)} %pack.1), calls=%async_computation | async-start | bytes 262144 | tf_op jit(solution)/shard_map/all_to_all | solution.py:424
  10.1 0.0 copy-start
  10.1 0.0 copy-start.1
  10.1 2.8 %resident.1 = bf16[8,64,128]{2,1,0:T(8,128)(2,1)} custom-call(s32[8]{0:T(128)} %len_hbm.1, bf16[8,256,128]{2,1,0:T(8,128)(2,1)} %bitcast.44, bf16[8,2,2,64]{3,2,1,0:T(2,128)(2,1)} %bitcast.51, bf16[8,64,128]{2,1,0:T(8,128)(2,1)} %bitcast.45, bf16[64,128]{1,0:T(8,128)(2,1)} %bitcast.49), custom_call_target="tpu_custom_call" | custom-call | flops 67108864 | bytes 786432 | tf_op jit(solution)/shard_map/resident/pallas_call | solution.py:360
  12.9 1.5 %all-to-all-done.got_ref = bf16[16,2,16,128]{3,2,1,0:T(8,128)(2,1)S(1)} async-done(((bf16[16,2,16,128]{3,2,1,0:T(8,128)(2,1)}), bf16[16,2,16,128]{3,2,1,0:T(8,128)(2,1)S(1)}, u32[]{:S(2)}, u32[]{:S(2)}) %all-to-all-start) | async-done | bytes 131104 | tf_op jit(solution)/shard_map/all_to_all | solution.py:424
  14.5 0.0 copy-done
  14.5 0.0 copy-done.1
  14.5 1.3 %arrivals.1 = bf16[6,2,32,128]{3,2,1,0:T(8,128)(2,1)} custom-call(bf16[16,2,16,128]{3,2,1,0:T(8,128)(2,1)S(1)} %all-to-all-done.got_ref, bf16[6,2,32,128]{3,2,1,0:T(8,128)(2,1)S(1)} %bitcast.42, bf16[48,128]{1,0:T(8,128)(2,1)S(1)} %bitcast.43), custom_call_target="tpu_custom_call" | custom-call | tf_op jit(solution)/shard_map/arrivals/pallas_call | solution.py:394
Async XLA Ops:
  2.3 12.1 %all-to-all-start = ((bf16[16,2,16,128]{3,2,1,0:T(8,128)(2,1)}), bf16[16,2,16,128]{3,2,1,0:T(8,128)(2,1)S(1)}, u32[]{:S(2)}, u32[]{:S(2)}) async-start(bf16[16,2,16,128]{3,2,1,0:T(8,128)(2,1)} %pack.1), calls=%async_computation | async-start | bytes 262144 | tf_op jit(solution)/shard_map/all_to_all | solution.py:424
  10.1 4.3 %copy-start = (bf16[6,2,4096]{2,1,0:T(2,128)(2,1)S(1)}, bf16[6,2,4096]{2,1,0:T(2,128)(2,1)}, u32[]{:S(2)}) copy-start(bf16[6,2,4096]{2,1,0:T(2,128)(2,1)} %param.20) | copy-start | bytes 294916
  10.1 4.3 %copy-start.1 = (bf16[6,2,2,256]{3,2,1,0:T(2,128)(2,1)S(1)}, bf16[6,2,2,256]{3,2,1,0:T(2,128)(2,1)}, u32[]{:S(2)}) copy-start(bf16[6,2,2,256]{3,2,1,0:T(2,128)(2,1)} %param.21) | copy-start | bytes 36868

commit v6 on v5

--- a/solution.py
+++ b/solution.py
@@ -419,7 +419,7 @@
     tp = lax.axis_size("tp")
     order = None
     if peers * tp == 16:
-        order = [11, 10, 12, 13, 14, 15, 3, 2, 1, 0, 5, 4, 7, 6, 9, 8]
+        order = [11, 10, 13, 12, 15, 14, 3, 2, 1, 0, 5, 4, 7, 6, 8, 9]
     send = pack(pre_codes, pre_scales, req_dest, req_blocks, peers, tp, order)
     got = lax.all_to_all(
         send,

time: 16 us -> 15.7 us (0.981)
  waiting for transfers between devices: 1.54 us -> 1.25 us
    all_to_all x1, waiting for transfers between devices: 1.54 us -> 1.25 us  [shards(): lax.all_to_all(send, ('wide', 'tp'), split_axis=0, concat_axis=0, tiled=T...]
where the time goes in v6:
time: 15.7 us; the launch traced here: 15.4 us
  starting transfers between devices  7.79 us (50%)
  Pallas kernels  5.73 us (36%)
  waiting for transfers between devices  1.25 us (8%)
  between operations  0.66 us (4%)
    all_to_all x1, starting transfers between devices, shards(): lax.all_to_all(send, ('wide', 'tp'), split_axis=0, concat_axis=0, tiled=T...  7.79 us
    pallas_call x1, Pallas kernels, resident(): pl.pallas_call(resident_kernel, out_shape=jax.ShapeDtypeStruct(query.shap...  2.78 us
    pallas_call x1, Pallas kernels, pack(): pl.pallas_call(functools.partial(pack_kernel, tp, order, KVH, 2 * block_t...  1.69 us
    pallas_call x1, Pallas kernels, arrivals(): pl.pallas_call(functools.partial(arrival_kernel, tp, groups, order, block...  1.26 us
    all_to_all x1, waiting for transfers between devices, shards(): lax.all_to_all(send, ('wide', 'tp'), split_axis=0, concat_axis=0, tiled=T...  1.25 us
  transfers between devices with their start and end apart: 1, of which 1 were waited for; matrix products, arithmetic and copies ran while one was open for 0% of the time, Pallas kernels for 18%

profile of v6, /device:TPU:0, one launch (start us, length us, event | category | flops | bytes accessed | tf_op | source)
XLA Modules:
  0.0 15.4 jit_solution(11039968160296773894)
XLA Ops:
  0.6 1.7 %pack.1 = bf16[16,2,16,128]{3,2,1,0:T(8,128)(2,1)} custom-call(s32[4]{0:T(128)} %dest_hbm.1, s32[4]{0:T(128)} %blocks_hbm.1, bf16[4,64,128]{2,1,0:T(8,128)(2,1)} %bitcast.48, bf16[4,16,4]{2,1,0:T(8,128)(2,1)} %bitcast.50), custom_call_target="tpu_custom_call" | custom-call | tf_op jit(solution)/shard_map/pack/pallas_call | solution.py:306
  2.3 7.8 %all-to-all-start = ((bf16[16,2,16,128]{3,2,1,0:T(8,128)(2,1)}), bf16[16,2,16,128]{3,2,1,0:T(8,128)(2,1)S(1)}, u32[]{:S(2)}, u32[]{:S(2)}) async-start(bf16[16,2,16,128]{3,2,1,0:T(8,128)(2,1)} %pack.1), calls=%async_computation | async-start | bytes 262144 | tf_op jit(solution)/shard_map/all_to_all | solution.py:424
  10.1 0.0 copy-start
  10.1 0.0 copy-start.1
  10.1 2.8 %resident.1 = bf16[8,64,128]{2,1,0:T(8,128)(2,1)} custom-call(s32[8]{0:T(128)} %len_hbm.1, bf16[8,256,128]{2,1,0:T(8,128)(2,1)} %bitcast.44, bf16[8,2,2,64]{3,2,1,0:T(2,128)(2,1)} %bitcast.51, bf16[8,64,128]{2,1,0:T(8,128)(2,1)} %bitcast.45, bf16[64,128]{1,0:T(8,128)(2,1)} %bitcast.49), custom_call_target="tpu_custom_call" | custom-call | flops 67108864 | bytes 786432 | tf_op jit(solution)/shard_map/resident/pallas_call | solution.py:360
  12.9 1.2 %all-to-all-done.got_ref = bf16[16,2,16,128]{3,2,1,0:T(8,128)(2,1)S(1)} async-done(((bf16[16,2,16,128]{3,2,1,0:T(8,128)(2,1)}), bf16[16,2,16,128]{3,2,1,0:T(8,128)(2,1)S(1)}, u32[]{:S(2)}, u32[]{:S(2)}) %all-to-all-start) | async-done | bytes 131104 | tf_op jit(solution)/shard_map/all_to_all | solution.py:424
  14.2 0.0 copy-done
  14.2 0.0 copy-done.1
  14.2 1.3 %arrivals.1 = bf16[6,2,32,128]{3,2,1,0:T(8,128)(2,1)} custom-call(bf16[16,2,16,128]{3,2,1,0:T(8,128)(2,1)S(1)} %all-to-all-done.got_ref, bf16[6,2,32,128]{3,2,1,0:T(8,128)(2,1)S(1)} %bitcast.42, bf16[48,128]{1,0:T(8,128)(2,1)S(1)} %bitcast.43), custom_call_target="tpu_custom_call" | custom-call | tf_op jit(solution)/shard_map/arrivals/pallas_call | solution.py:394
Async XLA Ops:
  2.3 11.8 %all-to-all-start = ((bf16[16,2,16,128]{3,2,1,0:T(8,128)(2,1)}), bf16[16,2,16,128]{3,2,1,0:T(8,128)(2,1)S(1)}, u32[]{:S(2)}, u32[]{:S(2)}) async-start(bf16[16,2,16,128]{3,2,1,0:T(8,128)(2,1)} %pack.1), calls=%async_computation | async-start | bytes 262144 | tf_op jit(solution)/shard_map/all_to_all | solution.py:424
  10.1 4.1 %copy-start = (bf16[6,2,4096]{2,1,0:T(2,128)(2,1)S(1)}, bf16[6,2,4096]{2,1,0:T(2,128)(2,1)}, u32[]{:S(2)}) copy-start(bf16[6,2,4096]{2,1,0:T(2,128)(2,1)} %param.20) | copy-start | bytes 294916
  10.1 4.1 %copy-start.1 = (bf16[6,2,2,256]{3,2,1,0:T(2,128)(2,1)S(1)}, bf16[6,2,2,256]{3,2,1,0:T(2,128)(2,1)}, u32[]{:S(2)}) copy-start(bf16[6,2,2,256]{3,2,1,0:T(2,128)(2,1)} %param.21) | copy-start | bytes 36868

commit v7 on v6

--- a/solution.py
+++ b/solution.py
@@ -419,7 +419,7 @@
     tp = lax.axis_size("tp")
     order = None
     if peers * tp == 16:
-        order = [11, 10, 13, 12, 15, 14, 3, 2, 1, 0, 5, 4, 7, 6, 8, 9]
+        order = [11, 10, 13, 12, 15, 14, 2, 3, 1, 0, 5, 4, 7, 6, 9, 8]
     send = pack(pre_codes, pre_scales, req_dest, req_blocks, peers, tp, order)
     got = lax.all_to_all(
         send,

time: 15.7 us -> 15.3 us (0.975)
  the two profiles are of different devices: /device:TPU:0 before, /device:TPU:1 now
where the time goes in v7:
time: 15.3 us; the launch traced here: 15.1 us
  starting transfers between devices  7.42 us (48%)
  Pallas kernels  5.73 us (37%)
  waiting for transfers between devices  1.24 us (8%)
  between operations  0.66 us (4%)
    all_to_all x1, starting transfers between devices, shards(): lax.all_to_all(send, ('wide', 'tp'), split_axis=0, concat_axis=0, tiled=T...  7.42 us
    pallas_call x1, Pallas kernels, resident(): pl.pallas_call(resident_kernel, out_shape=jax.ShapeDtypeStruct(query.shap...  2.78 us
    pallas_call x1, Pallas kernels, pack(): pl.pallas_call(functools.partial(pack_kernel, tp, order, KVH, 2 * block_t...  1.69 us
    pallas_call x1, Pallas kernels, arrivals(): pl.pallas_call(functools.partial(arrival_kernel, tp, groups, order, block...  1.27 us
    all_to_all x1, waiting for transfers between devices, shards(): lax.all_to_all(send, ('wide', 'tp'), split_axis=0, concat_axis=0, tiled=T...  1.24 us
  transfers between devices with their start and end apart: 1, of which 1 were waited for; matrix products, arithmetic and copies ran while one was open for 0% of the time, Pallas kernels for 18%

profile of v7, /device:TPU:1, one launch (start us, length us, event | category | flops | bytes accessed | tf_op | source)
XLA Modules:
  0.0 15.1 jit_solution(9288588930261620522)
XLA Ops:
  0.6 1.7 %pack.1 = bf16[16,2,16,128]{3,2,1,0:T(8,128)(2,1)} custom-call(s32[4]{0:T(128)} %dest_hbm.1, s32[4]{0:T(128)} %blocks_hbm.1, bf16[4,64,128]{2,1,0:T(8,128)(2,1)} %bitcast.48, bf16[4,16,4]{2,1,0:T(8,128)(2,1)} %bitcast.50), custom_call_target="tpu_custom_call" | custom-call | tf_op jit(solution)/shard_map/pack/pallas_call | solution.py:306
  2.3 7.4 %all-to-all-start = ((bf16[16,2,16,128]{3,2,1,0:T(8,128)(2,1)}), bf16[16,2,16,128]{3,2,1,0:T(8,128)(2,1)S(1)}, u32[]{:S(2)}, u32[]{:S(2)}) async-start(bf16[16,2,16,128]{3,2,1,0:T(8,128)(2,1)} %pack.1), calls=%async_computation | async-start | bytes 262144 | tf_op jit(solution)/shard_map/all_to_all | solution.py:424
  9.8 0.0 copy-start
  9.8 0.0 copy-start.1
  9.8 2.8 %resident.1 = bf16[8,64,128]{2,1,0:T(8,128)(2,1)} custom-call(s32[8]{0:T(128)} %len_hbm.1, bf16[8,256,128]{2,1,0:T(8,128)(2,1)} %bitcast.44, bf16[8,2,2,64]{3,2,1,0:T(2,128)(2,1)} %bitcast.51, bf16[8,64,128]{2,1,0:T(8,128)(2,1)} %bitcast.45, bf16[64,128]{1,0:T(8,128)(2,1)} %bitcast.49), custom_call_target="tpu_custom_call" | custom-call | flops 67108864 | bytes 786432 | tf_op jit(solution)/shard_map/resident/pallas_call | solution.py:360
  12.6 1.2 %all-to-all-done.got_ref = bf16[16,2,16,128]{3,2,1,0:T(8,128)(2,1)S(1)} async-done(((bf16[16,2,16,128]{3,2,1,0:T(8,128)(2,1)}), bf16[16,2,16,128]{3,2,1,0:T(8,128)(2,1)S(1)}, u32[]{:S(2)}, u32[]{:S(2)}) %all-to-all-start) | async-done | bytes 131104 | tf_op jit(solution)/shard_map/all_to_all | solution.py:424
  13.8 0.0 copy-done
  13.8 0.0 copy-done.1
  13.8 1.3 %arrivals.1 = bf16[6,2,32,128]{3,2,1,0:T(8,128)(2,1)} custom-call(bf16[16,2,16,128]{3,2,1,0:T(8,128)(2,1)S(1)} %all-to-all-done.got_ref, bf16[6,2,32,128]{3,2,1,0:T(8,128)(2,1)S(1)} %bitcast.42, bf16[48,128]{1,0:T(8,128)(2,1)S(1)} %bitcast.43), custom_call_target="tpu_custom_call" | custom-call | tf_op jit(solution)/shard_map/arrivals/pallas_call | solution.py:394
Async XLA Ops:
  2.3 11.5 %all-to-all-start = ((bf16[16,2,16,128]{3,2,1,0:T(8,128)(2,1)}), bf16[16,2,16,128]{3,2,1,0:T(8,128)(2,1)S(1)}, u32[]{:S(2)}, u32[]{:S(2)}) async-start(bf16[16,2,16,128]{3,2,1,0:T(8,128)(2,1)} %pack.1), calls=%async_computation | async-start | bytes 262144 | tf_op jit(solution)/shard_map/all_to_all | solution.py:424
  9.8 4.1 %copy-start = (bf16[6,2,4096]{2,1,0:T(2,128)(2,1)S(1)}, bf16[6,2,4096]{2,1,0:T(2,128)(2,1)}, u32[]{:S(2)}) copy-start(bf16[6,2,4096]{2,1,0:T(2,128)(2,1)} %param.20) | copy-start | bytes 294916
  9.8 4.0 %copy-start.1 = (bf16[6,2,2,256]{3,2,1,0:T(2,128)(2,1)S(1)}, bf16[6,2,2,256]{3,2,1,0:T(2,128)(2,1)}, u32[]{:S(2)}) copy-start(bf16[6,2,2,256]{3,2,1,0:T(2,128)(2,1)} %param.21) | copy-start | bytes 36868

commit v8 on v4

--- a/solution.py
+++ b/solution.py
@@ -115,7 +115,7 @@
         (len_hbm, len_ref), (codes_hbm, codes_ref),
     ]
     copies = [pltpu.make_async_copy(a, b, sems.at[i]) for i, (a, b) in enumerate(pairs)]
-    for copy in copies:
+    for copy in copies[:-1]:
         copy.start()
     slots, rows = codes_ref.shape[:2]
     heads = scales_ref.shape[2]
@@ -132,6 +132,7 @@
     )
     for copy in copies[:-1]:
         copy.wait()
+    copies[-1].start()
     flat = jnp.concatenate(
         [scales_ref[:, p, h] for p in range(2) for h in range(heads)], axis=1
     )

time: 15.3 us -> 15.4 us (level)
  Pallas kernels: 5.73 us -> 6.5 us
  waiting for transfers between devices: 1.24 us -> 0.48 us
    all_to_all x1, waiting for transfers between devices: 1.24 us -> 0.48 us  [shards(): lax.all_to_all(send, ('wide', 'tp'), split_axis=0, concat_axis=0, tiled=T...]
    pallas_call x1, Pallas kernels: 2.78 us -> 3.55 us  [resident(): pl.pallas_call(resident_kernel, out_shape=jax.ShapeDtypeStruct(query.shap...]
  transfers between devices with their start and end apart: 1 -> 1, of which waited for: 1 -> 1; matrix products, arithmetic and copies ran while one was open for 0% -> 0% of each run, Pallas kernels for 18% -> 23%
where the time goes in v8:
time: 15.4 us; the launch traced here: 15.1 us
  starting transfers between devices  7.42 us (48%)
  Pallas kernels  6.5 us (42%)
  between operations  0.66 us (4%)
  waiting for transfers between devices  0.48 us (3%)
    all_to_all x1, starting transfers between devices, shards(): lax.all_to_all(send, ('wide', 'tp'), split_axis=0, concat_axis=0, tiled=T...  7.42 us
    pallas_call x1, Pallas kernels, resident(): pl.pallas_call(resident_kernel, out_shape=jax.ShapeDtypeStruct(query.shap...  3.55 us
    pallas_call x1, Pallas kernels, pack(): pl.pallas_call(functools.partial(pack_kernel, tp, order, KVH, 2 * block_t...  1.69 us
    pallas_call x1, Pallas kernels, arrivals(): pl.pallas_call(functools.partial(arrival_kernel, tp, groups, order, block...  1.27 us
    all_to_all x1, waiting for transfers between devices, shards(): lax.all_to_all(send, ('wide', 'tp'), split_axis=0, concat_axis=0, tiled=T...  0.48 us
  transfers between devices with their start and end apart: 1, of which 1 were waited for; matrix products, arithmetic and copies ran while one was open for 0% of the time, Pallas kernels for 23%

profile of v8, /device:TPU:1, one launch (start us, length us, event | category | flops | bytes accessed | tf_op | source)
XLA Modules:
  0.0 15.1 jit_solution(13490088792718545633)
XLA Ops:
  0.6 1.7 %pack.1 = bf16[16,2,16,128]{3,2,1,0:T(8,128)(2,1)} custom-call(s32[4]{0:T(128)} %dest_hbm.1, s32[4]{0:T(128)} %blocks_hbm.1, bf16[4,64,128]{2,1,0:T(8,128)(2,1)} %bitcast.48, bf16[4,16,4]{2,1,0:T(8,128)(2,1)} %bitcast.50), custom_call_target="tpu_custom_call" | custom-call | tf_op jit(solution)/shard_map/pack/pallas_call | solution.py:307
  2.3 7.4 %all-to-all-start = ((bf16[16,2,16,128]{3,2,1,0:T(8,128)(2,1)}), bf16[16,2,16,128]{3,2,1,0:T(8,128)(2,1)S(1)}, u32[]{:S(2)}, u32[]{:S(2)}) async-start(bf16[16,2,16,128]{3,2,1,0:T(8,128)(2,1)} %pack.1), calls=%async_computation | async-start | bytes 262144 | tf_op jit(solution)/shard_map/all_to_all | solution.py:425
  9.8 0.0 copy-start
  9.8 0.0 copy-start.1
  9.8 3.5 %resident.1 = bf16[8,64,128]{2,1,0:T(8,128)(2,1)} custom-call(s32[8]{0:T(128)} %len_hbm.1, bf16[8,256,128]{2,1,0:T(8,128)(2,1)} %bitcast.44, bf16[8,2,2,64]{3,2,1,0:T(2,128)(2,1)} %bitcast.51, bf16[8,64,128]{2,1,0:T(8,128)(2,1)} %bitcast.45, bf16[64,128]{1,0:T(8,128)(2,1)} %bitcast.49), custom_call_target="tpu_custom_call" | custom-call | flops 67108864 | bytes 786432 | tf_op jit(solution)/shard_map/resident/pallas_call | solution.py:361
  13.3 0.5 %all-to-all-done.got_ref = bf16[16,2,16,128]{3,2,1,0:T(8,128)(2,1)S(1)} async-done(((bf16[16,2,16,128]{3,2,1,0:T(8,128)(2,1)}), bf16[16,2,16,128]{3,2,1,0:T(8,128)(2,1)S(1)}, u32[]{:S(2)}, u32[]{:S(2)}) %all-to-all-start) | async-done | bytes 131104 | tf_op jit(solution)/shard_map/all_to_all | solution.py:425
  13.8 0.0 copy-done
  13.8 0.0 copy-done.1
  13.8 1.3 %arrivals.1 = bf16[6,2,32,128]{3,2,1,0:T(8,128)(2,1)} custom-call(bf16[16,2,16,128]{3,2,1,0:T(8,128)(2,1)S(1)} %all-to-all-done.got_ref, bf16[6,2,32,128]{3,2,1,0:T(8,128)(2,1)S(1)} %bitcast.42, bf16[48,128]{1,0:T(8,128)(2,1)S(1)} %bitcast.43), custom_call_target="tpu_custom_call" | custom-call | tf_op jit(solution)/shard_map/arrivals/pallas_call | solution.py:395
Async XLA Ops:
  2.3 11.5 %all-to-all-start = ((bf16[16,2,16,128]{3,2,1,0:T(8,128)(2,1)}), bf16[16,2,16,128]{3,2,1,0:T(8,128)(2,1)S(1)}, u32[]{:S(2)}, u32[]{:S(2)}) async-start(bf16[16,2,16,128]{3,2,1,0:T(8,128)(2,1)} %pack.1), calls=%async_computation | async-start | bytes 262144 | tf_op jit(solution)/shard_map/all_to_all | solution.py:425
  9.8 4.1 %copy-start = (bf16[6,2,4096]{2,1,0:T(2,128)(2,1)S(1)}, bf16[6,2,4096]{2,1,0:T(2,128)(2,1)}, u32[]{:S(2)}) copy-start(bf16[6,2,4096]{2,1,0:T(2,128)(2,1)} %param.20) | copy-start | bytes 294916
  9.8 4.0 %copy-start.1 = (bf16[6,2,2,256]{3,2,1,0:T(2,128)(2,1)S(1)}, bf16[6,2,2,256]{3,2,1,0:T(2,128)(2,1)}, u32[]{:S(2)}) copy-start(bf16[6,2,2,256]{3,2,1,0:T(2,128)(2,1)} %param.21) | copy-start | bytes 36868
